TPU v7x, 32 devices: a whole 2x2x4 slice. The times are simulated.
32 devices in a mesh: attn: 8 (over y, x, core), expert: 4 (over z).
Axes of the slice: x: 2, y: 2, z: 4, core: 2. Of those that a mesh axis runs over, the one named last changes fastest.
Arguments:
- hidden: bfloat16 [4096, 2048], P(('attn', 'expert')), may hold values from -6 to 6
- queries: bfloat16 [4096, 4096], P(('attn', 'expert')), may hold values from -6 to 6
- new_keys: bfloat16 [4096, 512], P(('attn', 'expert')), may hold values from -6 to 6
- new_values: bfloat16 [4096, 512], P(('attn', 'expert')), may hold values from -6 to 6
- cache_keys: bfloat16 [32, 4096, 512], P(('attn', 'expert')), may hold values from -6 to 6
- cache_values: bfloat16 [32, 4096, 512], P(('attn', 'expert')), may hold values from -6 to 6
- option_ids: int32 [32, 128], P(('attn', 'expert')), may hold values from 0 to 3, never falling along the last dimension, each value on 1 to 64 neighbouring positions
- prompt_lengths: int32 [32], P(('attn', 'expert')), may hold values from 1 to 4096, 98304 in all
- query_gain: float32 [128], replicated, may hold values from 0.25 to 1.75
- key_gain: float32 [128], replicated, may hold values from 0.25 to 1.75
- out_proj: bfloat16 [4096, 2048], P('expert'), may hold values from -0.09375 to 0.09375
- post_gain: float32 [2048], replicated, may hold values from 0.25 to 1.75
- route_ids: int32 [4096, 8], P(('attn', 'expert')), may hold values from 0 to 31, all different within a row; in each aligned block of 128 rows (0 to 127, 128 to 255, ...) at most 48 rows name the same one
- route_weights: float32 [4096, 8], P(('attn', 'expert')), may hold values from 0.05 to 1
- expert_gate: bfloat16 [32, 2048, 768], P(('attn', 'expert')), may hold values from -0.125 to 0.125
- expert_up: bfloat16 [32, 2048, 768], P(('attn', 'expert')), may hold values from -0.125 to 0.125
- expert_down: bfloat16 [32, 768, 2048], P(('attn', 'expert')), may hold values from -0.21875 to 0.21875
Outputs:
- layer_out: bfloat16 [4096, 2048], P(('attn', 'expert'))
Inputs may be any that keep to these rules, and one draw needn't show every extreme that they name: `route_ids`: each row names 8 different experts. Among the 128 rows of one prompt (an aligned block of rows) no expert is named more than 48 times, and in every draw some expert is named exactly 48 times in some block. `option_ids`: along a prompt's 128 rows the option numbers never fall; each option holds 1 to 64 rows, and some option holds exactly 64. `prompt_lengths`: the lengths of all prompts sum to 98304, and the longest is exactly 4096.
All inputs are finite; a program needn't handle non-finite values. No bound on the sum of `prompt_lengths` on one device may be relied on, other than what follows from the above.
Results may differ from a plain program's by a relative error of at most 0.0095.
Values may be sent and summed in bfloat16 or wider, within the bound.
A program may use at most 128 MiB of HBM per device.

v0:
```python
import jax
import jax.numpy as jnp
from jax import lax
from jax.sharding import PartitionSpec as P

norm_eps = 1e-06


def rms_scaled(values, gain_row):
    mean_square = jnp.mean(values * values, axis=-1, keepdims=True)
    return values * lax.rsqrt(mean_square + norm_eps) * gain_row


def on_device(
    hidden,
    queries,
    new_keys,
    new_values,
    cache_keys,
    cache_values,
    option_ids,
    prompt_lengths,
    query_gain,
    key_gain,
    out_proj,
    post_gain,
    route_ids,
    route_weights,
    expert_gate,
    expert_up,
    expert_down,
):
    answer_rows = hidden.shape[0]
    model_width = hidden.shape[1]
    head_dim = query_gain.shape[0]
    key_heads = new_keys.shape[1] // head_dim
    query_heads = queries.shape[1] // head_dim
    groups = query_heads // key_heads
    prompt_len = cache_keys.shape[1]
    top_count = route_ids.shape[1]
    attn_count = lax.axis_size("attn")
    expert_count = lax.axis_size("expert")
    device_count = attn_count * expert_count
    capacity = 3 * answer_rows * top_count // (2 * device_count)
    merged_queries = rms_scaled(
        queries.astype(jnp.float32).reshape(answer_rows, key_heads, groups, head_dim), query_gain
    )
    merged_queries = (merged_queries * head_dim ** (-0.5)).astype(jnp.bfloat16)
    past_keys = rms_scaled(
        cache_keys[0].astype(jnp.float32).reshape(prompt_len, key_heads, head_dim), key_gain
    ).astype(jnp.bfloat16)
    past_values = cache_values[0].reshape(prompt_len, key_heads, head_dim)
    incoming_keys = rms_scaled(
        new_keys.astype(jnp.float32).reshape(answer_rows, key_heads, head_dim), key_gain
    ).astype(jnp.bfloat16)
    fresh_values = new_values.reshape(answer_rows, key_heads, head_dim)
    length = prompt_lengths[0]
    key_block = 512

    def add_past(block_index, running):
        first_key = block_index * key_block

        def visit_block(current):
            weighted_values, denominator = current
            key_block_slice = lax.dynamic_slice_in_dim(past_keys, first_key, key_block, 0)
            block_values = lax.dynamic_slice_in_dim(past_values, first_key, key_block, 0)
            logit_scores = jnp.einsum(
                "nfow,pfw->nfop",
                merged_queries,
                key_block_slice,
                preferred_element_type=jnp.float32,
            )
            visible = first_key + jnp.arange(key_block, dtype=jnp.int32) < length
            attention_weights = jnp.where(
                visible[None, None, None, :], jnp.exp(logit_scores), jnp.float32(0.0)
            )
            denominator = denominator + jnp.sum(attention_weights, axis=-1)
            weighted_values = weighted_values + jnp.einsum(
                "wvof,fvm->wvom",
                attention_weights.astype(jnp.bfloat16),
                block_values,
                preferred_element_type=jnp.float32,
            )
            return (weighted_values, denominator)

        return lax.cond(first_key < length, visit_block, lambda current: current, running)

    start_state = (
        jnp.zeros((answer_rows, key_heads, groups, head_dim), jnp.float32),
        jnp.zeros((answer_rows, key_heads, groups), jnp.float32),
    )
    weighted_values, denominator = lax.fori_loop(0, prompt_len // key_block, add_past, start_state)
    option_row = option_ids[0]
    positions = jnp.arange(answer_rows, dtype=jnp.int32)
    visible = (option_row[:, None] == option_row[None, :]) & (
        positions[None, :] <= positions[:, None]
    )
    logit_scores = jnp.einsum(
        "nfow,pfw->nfop", merged_queries, incoming_keys, preferred_element_type=jnp.float32
    )
    attention_weights = jnp.where(
        visible[:, None, None, :], jnp.exp(logit_scores), jnp.float32(0.0)
    )
    denominator = denominator + jnp.sum(attention_weights, axis=-1)
    weighted_values = weighted_values + jnp.einsum(
        "wvof,fvm->wvom",
        attention_weights.astype(jnp.bfloat16),
        fresh_values,
        preferred_element_type=jnp.float32,
    )
    attended = (
        (weighted_values / denominator[..., None])
        .reshape(answer_rows, query_heads * head_dim)
        .astype(jnp.bfloat16)
    )
    swapped = lax.all_to_all(attended, "expert", split_axis=1, concat_axis=0, tiled=True)
    projected = lax.psum_scatter(
        jnp.dot(swapped, out_proj, preferred_element_type=jnp.float32).astype(jnp.bfloat16),
        "expert",
        scatter_dimension=0,
        tiled=True,
    ).astype(jnp.float32)
    residual = (hidden.astype(jnp.float32) + projected).astype(jnp.bfloat16)
    normed = rms_scaled(residual.astype(jnp.float32), post_gain).astype(jnp.bfloat16)
    gate_share = route_weights / jnp.sum(route_weights, axis=1, keepdims=True)
    route_flat = route_ids.reshape(answer_rows * top_count)
    onehot = (route_flat[:, None] == jnp.arange(device_count, dtype=jnp.int32)[None, :]).astype(
        jnp.int32
    )
    slot_rank = jnp.sum((jnp.cumsum(onehot, axis=0) - onehot) * onehot, axis=1)
    target = route_flat * capacity + slot_rank
    outgoing = (
        jnp.zeros((device_count * capacity, model_width), jnp.bfloat16)
        .at[target]
        .set(jnp.repeat(normed, top_count, axis=0))
    )
    outgoing = outgoing.reshape(device_count, capacity, model_width)
    gate_matrix = expert_gate[0]
    up_matrix = expert_up[0]
    down_matrix = expert_down[0]
    arrived = lax.all_to_all(outgoing, ("attn", "expert"), split_axis=0, concat_axis=0, tiled=True)
    flat_rows = arrived.reshape(-1, model_width)
    gate_part = jnp.dot(flat_rows, gate_matrix, preferred_element_type=jnp.float32)
    up_part = jnp.dot(flat_rows, up_matrix, preferred_element_type=jnp.float32)
    activated = (jax.nn.silu(gate_part) * up_part).astype(jnp.bfloat16)
    returned = lax.all_to_all(
        jnp.dot(activated, down_matrix, preferred_element_type=jnp.float32)
        .astype(jnp.bfloat16)
        .reshape(arrived.shape),
        ("attn", "expert"),
        split_axis=0,
        concat_axis=0,
        tiled=True,
    )
    gathered = returned.reshape(device_count * capacity, model_width)[target].reshape(
        answer_rows, top_count, model_width
    )
    mixture = jnp.sum(gate_share[:, :, None] * gathered, axis=1)
    return (residual.astype(jnp.float32) + mixture).astype(jnp.bfloat16)


def solution(mesh):
    placed = (
        P(("attn", "expert"), None),
        P(("attn", "expert"), None),
        P(("attn", "expert"), None),
        P(("attn", "expert"), None),
        P(("attn", "expert"), None, None),
        P(("attn", "expert"), None, None),
        P(("attn", "expert"), None),
        P(("attn", "expert")),
        P(),
        P(),
        P("expert", None),
        P(),
        P(("attn", "expert"), None),
        P(("attn", "expert"), None),
        P(("attn", "expert"), None, None),
        P(("attn", "expert"), None, None),
        P(("attn", "expert"), None, None),
    )
    return jax.shard_map(
        on_device,
        mesh=mesh,
        in_specs=placed,
        out_specs=P(("attn", "expert"), None),
        check_vma=False,
    )
```

profile of v0, /device:TPU:5, one launch (start us, length us, event | category | flops | bytes accessed | tf_op | source)
XLA Modules:
  0.0 540.0 jit_solution(12730850377376697912)
XLA Ops:
  6.5 6.6 %copy.59 = bf16[1,4096,512]{1,2,0:T(8,128)(2,1)} copy(bf16[1,4096,512]{2,1,0:T(8,128)(2,1)} %param.26) | data formatting | bytes 8388608 | tf_op args[5]
  13.1 6.5 %copy.60 = bf16[1,4096,512]{1,2,0:T(8,128)(2,1)} copy(bf16[1,4096,512]{2,1,0:T(8,128)(2,1)} %param.25) | data formatting | bytes 8388608 | tf_op args[4]
  26.2 6.4 %copy.62 = bf16[4096,4,128]{2,0,1:T(8,128)(2,1)} copy(bf16[4096,4,128]{0,2,1:T(8,128)(2,1)} %fusion.13) | data formatting | bytes 8388608 | tf_op jit(solution)/shard_map/while | solution.py:92
  42.9 68.6 %while.15 = (s32[]{:T(128)}, f32[128,4,8,128]{0,3,2,1:T(8,128)}, f32[128,4,8]{0,2,1:T(8,128)S(1)}, s32[]{:T(128)}, bf16[4096,4,128]{0,2,1:T(8,128)(2,1)}, /*inde...) while((s32[]{:T(128)}, f32[128,4,8,128]{0,3,2,1:T(8,128)}, ...), condition=%wide.region_6.7_spmd, body=%wide.region_2.6_spmd.sunk | while | flops 1082655744 | bytes 39913288 | solution.py:92
  43.6 7.9 %conditional.2 = ((f32[128,4,8,128]{0,3,2,1:T(8,128)}, f32[128,4,8]{0,2,1:T(8,128)S(1)})) conditional(s32[]{:T(128)} %convert_element_type.158, (f32[128,4,8,128]{0,3,2,1:T(8,128)}, f32[128,4,8]{0,2,1:T(8,128)S(1)}) %tuple.42, (s32[]{:T(128)}, bf16[4096,4,128]{0,2,1:T(8,128)(2,1)}, s32[]{:T(128)}, bf16[4096,4,128]{2,0,1:T(8,128)(2,1)}, ...), branch_computations={%region_3.3_spmd, %region_4.5_spmd} | conditional | flops 1082655744 | bytes 39913088 | solution.py:86
  52.2 7.9 %conditional.2 = ((f32[128,4,8,128]{0,3,2,1:T(8,128)}, f32[128,4,8]{0,2,1:T(8,128)S(1)})) conditional(s32[]{:T(128)} %convert_element_type.158, (f32[128,4,8,128]{0,3,2,1:T(8,128)}, f32[128,4,8]{0,2,1:T(8,128)S(1)}) %tuple.42, (s32[]{:T(128)}, bf16[4096,4,128]{0,2,1:T(8,128)(2,1)}, s32[]{:T(128)}, bf16[4096,4,128]{2,0,1:T(8,128)(2,1)}, ...), branch_computations={%region_3.3_spmd, %region_4.5_spmd} | conditional | flops 1082655744 | bytes 39913088 | solution.py:86
  60.8 7.9 %conditional.2 = ((f32[128,4,8,128]{0,3,2,1:T(8,128)}, f32[128,4,8]{0,2,1:T(8,128)S(1)})) conditional(s32[]{:T(128)} %convert_element_type.158, (f32[128,4,8,128]{0,3,2,1:T(8,128)}, f32[128,4,8]{0,2,1:T(8,128)S(1)}) %tuple.42, (s32[]{:T(128)}, bf16[4096,4,128]{0,2,1:T(8,128)(2,1)}, s32[]{:T(128)}, bf16[4096,4,128]{2,0,1:T(8,128)(2,1)}, ...), branch_computations={%region_3.3_spmd, %region_4.5_spmd} | conditional | flops 1082655744 | bytes 39913088 | solution.py:86
  69.3 7.9 %conditional.2 = ((f32[128,4,8,128]{0,3,2,1:T(8,128)}, f32[128,4,8]{0,2,1:T(8,128)S(1)})) conditional(s32[]{:T(128)} %convert_element_type.158, (f32[128,4,8,128]{0,3,2,1:T(8,128)}, f32[128,4,8]{0,2,1:T(8,128)S(1)}) %tuple.42, (s32[]{:T(128)}, bf16[4096,4,128]{0,2,1:T(8,128)(2,1)}, s32[]{:T(128)}, bf16[4096,4,128]{2,0,1:T(8,128)(2,1)}, ...), branch_computations={%region_3.3_spmd, %region_4.5_spmd} | conditional | flops 1082655744 | bytes 39913088 | solution.py:86
  77.9 7.9 %conditional.2 = ((f32[128,4,8,128]{0,3,2,1:T(8,128)}, f32[128,4,8]{0,2,1:T(8,128)S(1)})) conditional(s32[]{:T(128)} %convert_element_type.158, (f32[128,4,8,128]{0,3,2,1:T(8,128)}, f32[128,4,8]{0,2,1:T(8,128)S(1)}) %tuple.42, (s32[]{:T(128)}, bf16[4096,4,128]{0,2,1:T(8,128)(2,1)}, s32[]{:T(128)}, bf16[4096,4,128]{2,0,1:T(8,128)(2,1)}, ...), branch_computations={%region_3.3_spmd, %region_4.5_spmd} | conditional | flops 1082655744 | bytes 39913088 | solution.py:86
  86.4 7.9 %conditional.2 = ((f32[128,4,8,128]{0,3,2,1:T(8,128)}, f32[128,4,8]{0,2,1:T(8,128)S(1)})) conditional(s32[]{:T(128)} %convert_element_type.158, (f32[128,4,8,128]{0,3,2,1:T(8,128)}, f32[128,4,8]{0,2,1:T(8,128)S(1)}) %tuple.42, (s32[]{:T(128)}, bf16[4096,4,128]{0,2,1:T(8,128)(2,1)}, s32[]{:T(128)}, bf16[4096,4,128]{2,0,1:T(8,128)(2,1)}, ...), branch_computations={%region_3.3_spmd, %region_4.5_spmd} | conditional | flops 1082655744 | bytes 39913088 | solution.py:86
  95.0 7.9 %conditional.2 = ((f32[128,4,8,128]{0,3,2,1:T(8,128)}, f32[128,4,8]{0,2,1:T(8,128)S(1)})) conditional(s32[]{:T(128)} %convert_element_type.158, (f32[128,4,8,128]{0,3,2,1:T(8,128)}, f32[128,4,8]{0,2,1:T(8,128)S(1)}) %tuple.42, (s32[]{:T(128)}, bf16[4096,4,128]{0,2,1:T(8,128)(2,1)}, s32[]{:T(128)}, bf16[4096,4,128]{2,0,1:T(8,128)(2,1)}, ...), branch_computations={%region_3.3_spmd, %region_4.5_spmd} | conditional | flops 1082655744 | bytes 39913088 | solution.py:86
  103.6 7.9 %conditional.2 = ((f32[128,4,8,128]{0,3,2,1:T(8,128)}, f32[128,4,8]{0,2,1:T(8,128)S(1)})) conditional(s32[]{:T(128)} %convert_element_type.158, (f32[128,4,8,128]{0,3,2,1:T(8,128)}, f32[128,4,8]{0,2,1:T(8,128)S(1)}) %tuple.42, (s32[]{:T(128)}, bf16[4096,4,128]{0,2,1:T(8,128)(2,1)}, s32[]{:T(128)}, bf16[4096,4,128]{2,0,1:T(8,128)(2,1)}, ...), branch_computations={%region_3.3_spmd, %region_4.5_spmd} | conditional | flops 1082655744 | bytes 39913088 | solution.py:86
  120.0 29.5 %all_to_all.26 = bf16[128,4,1024]{2,0,1:T(8,128)(2,1)S(1)} all-to-all(bf16[128,4,1024]{2,0,1:T(8,128)(2,1)} %copy.70), channel_id=1, replica_groups=mesh['attn'=8,'expert'=4] {'expert'}, dimensions={1} | all-to-all | bytes 2097152 | tf_op jit(solution)/shard_map/all_to_all | solution.py:116
  149.5 5.9 %convolution_convert_fusion.1 = bf16[512,2048]{1,0:T(8,128)(2,1)} fusion(bf16[512,1024]{1,0:T(8,128)(2,1)S(1)} %bitcast.108, bf16[1024,2048]{1,0:T(8,128)(2,1)} %param.31), kind=kOutput, calls=%fused_computation.34 | convolution fusion | flops 2148532224 | bytes 7340032 | tf_op jit(solution)/shard_map/dot_general | solution.py:118
  155.9 9.0 %reduce-window.6 = s32[32,8,128]{2,1,0:T(8,128)S(1)} reduce-window(s32[32,8,128]{2,1,0:T(8,128)S(1)} %fusion.44, s32[]{:T(128)} %constant.31.clone.1), window={size=1x1x128 pad=0_0x0_0x127_0}, to_apply=%region_11.12 | reduce-window | flops 4161536 | bytes 262148 | tf_op jit(solution)/shard_map/reduce-window
  165.4 33.2 %reduce-scatter.2.cloned.1.call-done = bf16[128,2048]{1,0:T(8,128)(2,1)} async-done(((bf16[512,2048]{1,0:T(8,128)(2,1)}), bf16[128,2048]{1,0:T(8,128)(2,1)}) %reduce-scatter.2.cloned.1.call-update) | async-done | bytes 524304 | tf_op jit(solution)/shard_map/reduce_scatter | solution.py:117
  202.4 10.7 %scatter_custom_fusion = bf16[1536,2048]{1,0:T(8,128)(2,1)} fusion(s32[1024]{0:T(1024)S(1)} %bitcast.113, bf16[]{:T(256)} %constant.54.clone.1, bf16[128,2048]{1,0:T(8,128)(2,1)} %fusion.33), kind=kCustom, calls=%fused_computation.27 | custom fusion | bytes 6815746 | tf_op jit(solution)/shard_map/scatter | solution.py:135
  213.0 143.2 %all_to_all.27 = bf16[32,48,2048]{2,1,0:T(8,128)(2,1)S(1)} all-to-all(bf16[32,48,2048]{2,1,0:T(8,128)(2,1)} %bitcast.102), channel_id=1, replica_groups=mesh['attn'=8,'expert'=4] {'attn','expert'}, dimensions={0} | all-to-all | bytes 12582912 | tf_op jit(solution)/shard_map/all_to_all | solution.py:141
  356.2 5.2 fusion.19
  361.5 5.6 %multiply_convert_fusion = bf16[1536,768]{1,0:T(8,128)(2,1)S(1)} fusion(f32[1536,768]{1,0:T(8,128)S(1)} %fusion.19, bf16[1536,2048]{1,0:T(8,128)(2,1)S(1)} %bitcast.106, bf16[1,2048,768]{2,1,0:T(8,128)(2,1)S(1)} %copy-done.18), kind=kOutput, calls=%fused_computation.26 | convolution fusion | flops 4838916096 | bytes 16515072 | tf_op jit(solution)/shard_map/dot_general | solution.py:144
  367.1 7.0 %convolution_convert_fusion = bf16[1536,2048]{1,0:T(8,128)(2,1)} fusion(bf16[1536,768]{1,0:T(8,128)(2,1)S(1)} %multiply_convert_fusion, bf16[1,768,2048]{2,1,0:T(8,128)(2,1)S(1)} %copy-done), kind=kOutput, calls=%fused_computation.25 | convolution fusion | flops 4834983936 | bytes 11796480 | tf_op jit(solution)/shard_map/dot_general | solution.py:147
  378.0 135.2 %all-to-all-done.2 = bf16[32,48,2048]{2,1,0:T(8,128)(2,1)} async-done(((bf16[32,48,2048]{2,1,0:T(8,128)(2,1)}), bf16[32,48,2048]{2,1,0:T(8,128)(2,1)}, u32[]{:S(2)}, u32[]{:S(2)}) %all-to-all-start.2) | async-done | bytes 6291488 | tf_op jit(solution)/shard_map/all_to_all | solution.py:146
  513.2 12.4 %gather_fusion = bf16[1024,2048]{1,0:T(8,128)(2,1)} fusion(bf16[1536,2048]{1,0:T(8,128)(2,1)} %bitcast.33, s32[1024]{0:T(1024)S(1)} %broadcast_clamp_fusion), kind=kCustom, calls=%fused_computation | custom fusion | bytes 8392704 | tf_op jit(solution)/shard_map/gather | solution.py:155
  525.6 6.6 %fusion.14 = f32[128,2048]{1,0:T(8,128)S(1)} fusion(bf16[1024,2048]{1,0:T(8,128)(2,1)} %gather_fusion, f32[128,8]{1,0:T(8,128)S(1)} %copy.71), kind=kLoop, calls=%fused_computation.24 | loop fusion | flops 6029312 | bytes 5246976 | tf_op jit(solution)/shard_map/reduce_sum | solution.py:158
  (144 shorter events, 97.6 us)
Async XLA Ops:
  6.5 360.5 %copy-start = (bf16[1,768,2048]{2,1,0:T(8,128)(2,1)S(1)}, bf16[1,768,2048]{2,1,0:T(8,128)(2,1)}, u32[]{:S(2)}) copy-start(bf16[1,768,2048]{2,1,0:T(8,128)(2,1)} %param.37) | copy-start | bytes 9437188
  6.5 192.2 %reduce-scatter.2.cloned.1.call-start = ((), (), s32[]{:S(2)}) async-start(), calls=%async_computation.4 | async-start | bytes 2621440 | tf_op jit(solution)/shard_map/reduce_scatter | solution.py:117
  19.5 3.4 copy-start.4
  19.6 3.4 copy-start.15
  26.2 10.2 %copy-start.16 = (f32[128]{0:T(128)S(1)}, f32[128]{0:T(128)}, u32[]{:S(2)}) copy-start(f32[128]{0:T(128)} %param.29) | copy-start | bytes 1540
  42.9 68.6 %copy-start.8 = (bf16[128,512]{1,0:T(8,128)(2,1)S(1)}, bf16[128,512]{1,0:T(8,128)(2,1)}, u32[]{:S(2)}) copy-start(bf16[128,512]{1,0:T(8,128)(2,1)} %param.24) | copy-start | bytes 393220
  42.9 69.3 %copy-start.14 = (s32[1,128]{1,0:T(1,128)S(1)}, s32[1,128]{1,0:T(1,128)}, u32[]{:S(2)}) copy-start(s32[1,128]{1,0:T(1,128)} %param.27) | copy-start | bytes 1540
  42.9 70.0 %copy-start.7 = (bf16[128,512]{1,0:T(8,128)(2,1)S(1)}, bf16[128,512]{1,0:T(8,128)(2,1)}, u32[]{:S(2)}) copy-start(bf16[128,512]{1,0:T(8,128)(2,1)} %param.23) | copy-start | bytes 393220
  52.9 3.0 copy-start.1
  61.4 3.0 copy-start.1
  70.0 3.0 copy-start.1
  78.6 3.0 copy-start.1
  87.1 3.0 copy-start.1
  95.7 3.0 copy-start.1
  104.3 3.0 copy-start.1
  113.0 3.0 copy-start.3
  149.4 5.9 %copy-start.11 = (s32[128,8]{0,1:T(8,128)S(1)}, s32[128,8]{0,1:T(8,128)}, u32[]{:S(2)}) copy-start(s32[128,8]{0,1:T(8,128)} %param.33) | copy-start | bytes 12292
  155.4 44.8 %copy-start.13 = (f32[2048]{0:T(1024)S(1)}, f32[2048]{0:T(1024)}, u32[]{:S(2)}) copy-start(f32[2048]{0:T(1024)} %param.32) | copy-start | bytes 24580
  213.0 143.2 %copy-start.17 = (bf16[1,2048,768]{2,1,0:T(8,128)(2,1)S(1)}, bf16[1,2048,768]{2,1,0:T(8,128)(2,1)}, u32[]{:S(2)}) copy-start(bf16[1,2048,768]{2,1,0:T(8,128)(2,1)} %param.35) | copy-start | bytes 9437188
  356.2 5.2 copy-start.18
  374.1 3.8 copy-start.12
  374.1 139.1 %all-to-all-start.2 = ((bf16[32,48,2048]{2,1,0:T(8,128)(2,1)}), bf16[32,48,2048]{2,1,0:T(8,128)(2,1)}, u32[]{:S(2)}, u32[]{:S(2)}) async-start(bf16[32,48,2048]{2,1,0:T(8,128)(2,1)} %bitcast.104), calls=%async_computation.3 | async-start | bytes 12582912 | tf_op jit(solution)/shard_map/all_to_all | solution.py:146
  525.6 6.6 %copy-start.5 = (bf16[128,2048]{1,0:T(8,128)(2,1)S(1)}, bf16[128,2048]{1,0:T(8,128)(2,1)}, u32[]{:S(2)}) copy-start(bf16[128,2048]{1,0:T(8,128)(2,1)} %param.21) | copy-start | bytes 1572868
  525.6 6.6 %copy-start.6 = (bf16[128,2048]{1,0:T(8,128)(2,1)S(1)}, bf16[128,2048]{1,0:T(8,128)(2,1)}, u32[]{:S(2)}) copy-start(bf16[128,2048]{1,0:T(8,128)(2,1)} %reduce-scatter.2.cloned.1.call-done) | copy-start | bytes 1572868
  (11 other events, 20.3 us)
Sparse Core Ops, SparseCore 0:
  155.5 43.1 reduce-scatter.1
where the time goes:
time: 545 us; the launch traced here: 540 us
  blocking collectives  173 us (32%)
  waiting for transfers between devices  168 us (31%)
  matrix products  73.4 us (13%)
  local copies, waits for them, and re-layouts  64 us (12%)
  other arithmetic  38.2 us (7%)
  between operations  13.7 us (3%)
  loops' own time  5.83 us (1%)
    all_to_all x1, blocking collectives, on_device(): lax.all_to_all(outgoing, ('attn', 'expert'), split_axis=0, concat_axis=0,...  143 us
    all_to_all x1, waiting for transfers between devices, on_device(): lax.all_to_all(jnp.dot(activated, down_matrix, preferred_element_type=jnp...  135 us
    reduce_scatter x1, waiting for transfers between devices, on_device(): lax.psum_scatter(jnp.dot(swapped, out_proj, preferred_element_type=jnp.fl...  33.2 us
    all_to_all x1, blocking collectives, on_device(): lax.all_to_all(attended, 'expert', split_axis=1, concat_axis=0, tiled=True)  29.5 us
    dot_general x8, matrix products, visit_block(): jnp.einsum('nfow,pfw->nfop', merged_queries, key_block_slice, preferred_e...  24.2 us
    dot_general x8, matrix products, visit_block(): jnp.einsum('wvof,fvm->wvom', attention_weights.astype(jnp.bfloat16), bloc...  22.1 us
    unnamed x38, local copies, waits for them, and re-layouts  15.6 us
    gather x1, local copies, waits for them, and re-layouts, on_device(): returned.reshape(device_count * capacity, model_width)[target]  12.4 us
  transfers between devices with their start and end apart: 2, of which 2 were waited for; matrix products, arithmetic and copies ran while one was open for 2% of the time, Pallas kernels for 0%

commit v1 on v0

v1 whole, which is shorter than its diff:
```python
import functools

import jax
import jax.numpy as jnp
from jax import lax
from jax.experimental import pallas as pl
from jax.experimental.pallas import tpu as pltpu
from jax.sharding import PartitionSpec as P

norm_eps = 1e-06
log2_e = 1.4426950408889634


def rms_scaled(values, gain_row):
    mean_square = jnp.mean(values * values, axis=-1, keepdims=True)
    return values * lax.rsqrt(mean_square + norm_eps) * gain_row


def attention_kernel(
    key_block,
    length_ref,
    query_ref,
    new_key_ref,
    new_value_ref,
    past_key_ref,
    past_value_ref,
    option_row_ref,
    option_column_ref,
    query_gain_ref,
    key_gain_ref,
    out_ref,
    query_unit,
    total,
):
    head_dim = query_gain_ref.shape[1]
    answer_rows = query_ref.shape[0]
    groups = query_ref.shape[1] // head_dim
    query_gain = query_gain_ref[...] * (head_dim ** (-0.5) * log2_e)
    key_gain = key_gain_ref[...]
    for group in range(groups):
        rows = query_ref[:, group * head_dim : (group + 1) * head_dim].astype(jnp.float32)
        query_unit[group * answer_rows : (group + 1) * answer_rows, :] = rms_scaled(
            rows, query_gain
        ).astype(jnp.bfloat16)

    def block_sum(keys, values, visible):
        keys = rms_scaled(keys.astype(jnp.float32), key_gain).astype(jnp.bfloat16)
        scores = lax.dot_general(
            query_unit[...], keys, (((1,), (1,)), ((), ())), preferred_element_type=jnp.float32
        )
        weights = jnp.exp2(scores)
        if visible is not None:
            weights = jnp.where(visible, weights, 0.0)
        wide = jnp.concatenate([values, jnp.ones_like(values)], axis=1)
        return jnp.dot(weights.astype(jnp.bfloat16), wide, preferred_element_type=jnp.float32)

    position_row = lax.broadcasted_iota(jnp.int32, (answer_rows, answer_rows), 0)
    position_column = lax.broadcasted_iota(jnp.int32, (answer_rows, answer_rows), 1)
    fresh = ((option_column_ref[...] == option_row_ref[...]) & (position_column <= position_row)).astype(
        jnp.float32
    )
    fresh = jnp.concatenate([fresh] * groups, axis=0) > 0.5
    total[...] = block_sum(new_key_ref[...], new_value_ref[...], fresh)
    length = length_ref[0]
    whole = length // key_block

    @pl.loop(0, whole)
    def _(index):
        here = pl.ds(pl.multiple_of(index * key_block, key_block), key_block)
        total[...] += block_sum(past_key_ref[here, :], past_value_ref[here, :], None)

    @pl.when(whole * key_block < length)
    def _():
        first = pl.multiple_of(whole * key_block, key_block)
        here = pl.ds(first, key_block)
        visible = first + lax.broadcasted_iota(jnp.int32, (1, key_block), 1) < length
        total[...] += block_sum(past_key_ref[here, :], past_value_ref[here, :], visible)

    for group in range(groups):
        rows = slice(group * answer_rows, (group + 1) * answer_rows)
        out_ref[:, group * head_dim : (group + 1) * head_dim] = (
            total[rows, :head_dim] / total[rows, head_dim:]
        ).astype(jnp.bfloat16)


def attend(
    queries,
    new_keys,
    new_values,
    past_keys,
    past_values,
    option_ids,
    length,
    query_gain,
    key_gain,
):
    answer_rows = queries.shape[0]
    head_dim = query_gain.shape[0]
    prompt_len = past_keys.shape[0]
    key_heads = new_keys.shape[1] // head_dim
    group_width = queries.shape[1] // key_heads
    groups = group_width // head_dim
    key_block = min(512, prompt_len)

    def by_head(rows, width):
        return pl.BlockSpec((rows, width), lambda head, length: (0, head))

    def fixed(rows, width):
        return pl.BlockSpec((rows, width), lambda head, length: (0, 0))

    return pl.pallas_call(
        functools.partial(attention_kernel, key_block),
        out_shape=jax.ShapeDtypeStruct(queries.shape, jnp.bfloat16),
        grid_spec=pltpu.PrefetchScalarGridSpec(
            num_scalar_prefetch=1,
            grid=(key_heads,),
            in_specs=[
                by_head(answer_rows, group_width),
                by_head(answer_rows, head_dim),
                by_head(answer_rows, head_dim),
                by_head(prompt_len, head_dim),
                by_head(prompt_len, head_dim),
                fixed(1, answer_rows),
                fixed(answer_rows, 1),
                fixed(1, head_dim),
                fixed(1, head_dim),
            ],
            out_specs=by_head(answer_rows, group_width),
            scratch_shapes=[
                pltpu.VMEM((groups * answer_rows, head_dim), jnp.bfloat16),
                pltpu.VMEM((groups * answer_rows, 2 * head_dim), jnp.float32),
            ],
        ),
        compiler_params=pltpu.CompilerParams(vmem_limit_bytes=32 * 2**20),
        cost_estimate=pl.CostEstimate(
            flops=4 * queries.size * prompt_len,
            bytes_accessed=4 * past_keys.size,
            transcendentals=queries.size // head_dim * prompt_len,
        ),
        name="attend",
    )(
        length,
        queries,
        new_keys,
        new_values,
        past_keys,
        past_values,
        option_ids,
        option_ids.reshape(answer_rows, 1),
        query_gain.reshape(1, head_dim),
        key_gain.reshape(1, head_dim),
    )


def on_device(
    hidden,
    queries,
    new_keys,
    new_values,
    cache_keys,
    cache_values,
    option_ids,
    prompt_lengths,
    query_gain,
    key_gain,
    out_proj,
    post_gain,
    route_ids,
    route_weights,
    expert_gate,
    expert_up,
    expert_down,
):
    answer_rows, model_width = hidden.shape
    top_count = route_ids.shape[1]
    attn_count = lax.axis_size("attn")
    expert_count = lax.axis_size("expert")
    device_count = attn_count * expert_count
    capacity = 3 * answer_rows * top_count // (2 * device_count)
    capacity = (capacity + 15) // 16 * 16
    plane = lax.axis_index("expert")

    gate_share = route_weights / jnp.sum(route_weights, axis=1, keepdims=True)
    ids = lax.all_gather(route_ids, "expert")
    shares = lax.all_gather(gate_share, "expert")
    plane_experts = jnp.arange(attn_count, dtype=jnp.int32) * expert_count + plane
    chosen = ids[:, None, :, :] == plane_experts[None, :, None, None]
    share = jnp.sum(jnp.where(chosen, shares[:, None, :, :], 0.0), axis=-1)
    hit = jnp.any(chosen, axis=-1)
    earlier = (
        jnp.arange(answer_rows)[:, None] < jnp.arange(answer_rows)[None, :]
    ).astype(jnp.bfloat16)
    rank = jnp.einsum(
        "ear,rs->eas", hit.astype(jnp.bfloat16), earlier, preferred_element_type=jnp.float32
    ).astype(jnp.int32)
    slot = jnp.where(hit, rank, -1)
    picks = slot[:, :, None, :] == jnp.arange(capacity, dtype=jnp.int32)[None, None, :, None]
    select = picks.astype(jnp.bfloat16)
    combine = jnp.where(picks, share[:, :, None, :], 0.0).astype(jnp.bfloat16)

    attended = attend(
        queries,
        new_keys,
        new_values,
        cache_keys[0],
        cache_values[0],
        option_ids,
        prompt_lengths,
        query_gain,
        key_gain,
    )
    swapped = lax.all_to_all(attended, "expert", split_axis=1, concat_axis=0, tiled=True)
    projected = lax.psum_scatter(
        jnp.dot(swapped, out_proj, preferred_element_type=jnp.float32).astype(jnp.bfloat16),
        "expert",
        scatter_dimension=0,
        tiled=True,
    ).astype(jnp.float32)
    residual = (hidden.astype(jnp.float32) + projected).astype(jnp.bfloat16)
    normed = rms_scaled(residual.astype(jnp.float32), post_gain).astype(jnp.bfloat16)

    column = lax.all_gather(normed, "expert")
    outgoing = jnp.einsum(
        "eacr,erd->aecd", select, column, preferred_element_type=jnp.float32
    ).astype(jnp.bfloat16)
    arrived = lax.all_to_all(outgoing, "attn", split_axis=0, concat_axis=0, tiled=True)
    flat_rows = arrived.reshape(-1, model_width)
    gate_part = jnp.dot(flat_rows, expert_gate[0], preferred_element_type=jnp.float32)
    up_part = jnp.dot(flat_rows, expert_up[0], preferred_element_type=jnp.float32)
    activated = (jax.nn.silu(gate_part) * up_part).astype(jnp.bfloat16)
    returned = lax.all_to_all(
        jnp.dot(activated, expert_down[0], preferred_element_type=jnp.float32)
        .astype(jnp.bfloat16)
        .reshape(arrived.shape),
        "attn",
        split_axis=0,
        concat_axis=0,
        tiled=True,
    )
    partial = jnp.einsum(
        "eacr,aecd->erd", combine, returned, preferred_element_type=jnp.float32
    ).astype(jnp.bfloat16)
    mixture = lax.psum_scatter(partial, "expert", scatter_dimension=0, tiled=True)[0]
    return (residual.astype(jnp.float32) + mixture.astype(jnp.float32)).astype(jnp.bfloat16)


def solution(mesh):
    rows = P(("attn", "expert"), None)
    blocks = P(("attn", "expert"), None, None)
    placed = (
        rows,
        rows,
        rows,
        rows,
        blocks,
        blocks,
        rows,
        P(("attn", "expert")),
        P(),
        P(),
        P("expert", None),
        P(),
        rows,
        rows,
        blocks,
        blocks,
        blocks,
    )
    return jax.shard_map(
        on_device,
        mesh=mesh,
        in_specs=placed,
        out_specs=rows,
        check_vma=False,
    )
```

time: 545 us -> 409 us (0.75)
  local copies, waits for them, and re-layouts: 64 us -> 11.5 us
  blocking collectives: 173 us -> 125 us
  matrix products: 73.4 us -> 30.6 us
  Pallas kernels: 0 us -> 33.7 us
  other arithmetic: 38.2 us -> 6.32 us
  waiting for transfers between devices: 168 us -> 178 us
  loops' own time: 5.83 us -> 0 us
    all_to_all x1, waiting for transfers between devices: 135 us -> 57.4 us  [on_device(): lax.all_to_all(jnp.dot(activated, expert_down[0], preferred_element_type=...]
    all_to_all x1, blocking collectives: 143 us -> 73.7 us  [on_device(): lax.all_to_all(outgoing, 'attn', split_axis=0, concat_axis=0, tiled=True)]
    reduce_scatter x0 -> x1, waiting for transfers between devices: none -> 43.8 us  [on_device(): lax.psum_scatter(partial, 'expert', scatter_dimension=0, tiled=True)[0]]
    dot_general x21 -> x6, matrix products: 67.5 us -> 26.9 us  [the longest x1 7.08 us: on_device(): jnp.dot(activated, expert_down[0], preferred_element_type=jnp.float32)]
    all_gather x0 -> x1, waiting for transfers between devices: none -> 35.1 us  [on_device(): column = lax.all_gather(normed, 'expert')]
    pallas_call x0 -> x1, Pallas kernels: none -> 33.7 us  [attend(): pl.pallas_call(functools.partial(attention_kernel, key_block), out_shape=...]
    all_gather x0 -> x2, blocking collectives: none -> 20.5 us  [the longest x1 10.2 us: on_device(): ids = lax.all_gather(route_ids, 'expert')]
    gather x1 -> x0, local copies, waits for them, and re-layouts: 12.4 us -> none  [on_device(): returned.reshape(device_count * capacity, model_width)[target]]
  transfers between devices with their start and end apart: 2 -> 4, of which waited for: 2 -> 4; matrix products, arithmetic and copies ran while one was open for 2% -> 0% of each run, Pallas kernels for 0% -> 0%
where the time goes in v1:
time: 409 us; the launch traced here: 407 us
  waiting for transfers between devices  178 us (44%)
  blocking collectives  125 us (31%)
  Pallas kernels  33.7 us (8%)
  matrix products  30.6 us (7%)
  between operations  14 us (3%)
  local copies, waits for them, and re-layouts  11.5 us (3%)
  starting transfers between devices  7.24 us (2%)
  other arithmetic  6.32 us (2%)
    all_to_all x1, blocking collectives, on_device(): lax.all_to_all(outgoing, 'attn', split_axis=0, concat_axis=0, tiled=True)  73.7 us
    all_to_all x1, waiting for transfers between devices, on_device(): lax.all_to_all(jnp.dot(activated, expert_down[0], preferred_element_type=...  57.4 us
    reduce_scatter x1, waiting for transfers between devices, on_device(): lax.psum_scatter(partial, 'expert', scatter_dimension=0, tiled=True)[0]  43.8 us
    reduce_scatter x1, waiting for transfers between devices, on_device(): lax.psum_scatter(jnp.dot(swapped, out_proj, preferred_element_type=jnp.fl...  42 us
    all_gather x1, waiting for transfers between devices, on_device(): column = lax.all_gather(normed, 'expert')  35.1 us
    pallas_call x1, Pallas kernels, attend(): pl.pallas_call(functools.partial(attention_kernel, key_block), out_shape=...  33.7 us
    all_to_all x1, blocking collectives, on_device(): lax.all_to_all(attended, 'expert', split_axis=1, concat_axis=0, tiled=True)  30.6 us
    all_gather x1, blocking collectives, on_device(): ids = lax.all_gather(route_ids, 'expert')  10.2 us
  transfers between devices with their start and end apart: 4, of which 4 were waited for; matrix products, arithmetic and copies ran while one was open for 0% of the time, Pallas kernels for 0%

profile of v1, /device:TPU:5, one launch (start us, length us, event | category | flops | bytes accessed | tf_op | source)
XLA Modules:
  0.0 406.5 jit_solution(5916100108059741297)
XLA Ops:
  7.3 0.9 copy.34.option_column_ref
  8.9 2.2 copy-done.2
  11.1 2.2 copy-done.3
  13.3 1.2 copy-done.4
  17.6 33.7 %attend.1 = bf16[128,4096]{1,0:T(8,128)(2,1)S(1)} custom-call(s32[1]{0:T(128)S(6)} %copy.47.length_ref, bf16[128,4096]{1,0:T(8,128)(2,1)S(1)} %copy-done.4, bf16[128,512]{1,0:T(8,128)(2,1)S(1)} %copy-done.5, bf16[128,512]{1,0:T(8,128)(2,1)S(1)} %copy-done.6, bf16[4096,512]{1,0:T(8,128)(2,1)S(1)} %bitcast.50, bf16[4096,512]{1,0:T(8,128)(2,1)S(1)} %bitcast.51, ...), custom_call_target="tpu_custom_call" | custom-call | flops 8589934592 | bytes 8388608 | tf_op jit(solution)/shard_map/attend/pallas_call | solution.py:111
  51.4 30.6 %all_to_all.29 = bf16[128,4,1024]{2,0,1:T(8,128)(2,1)S(1)} all-to-all(bf16[128,4,1024]{2,0,1:T(8,128)(2,1)S(1)} %bitcast.57), channel_id=1, replica_groups=mesh['attn'=8,'expert'=4] {'expert'}, dimensions={1} | all-to-all | bytes 2097152 | tf_op jit(solution)/shard_map/all_to_all | solution.py:212
  82.1 3.7 convolution_convert_fusion.1
  85.8 42.0 %reduce-scatter.3.cloned.1.call-done = bf16[128,2048]{1,0:T(8,128)(2,1)} async-done(((bf16[512,2048]{1,0:T(8,128)(2,1)}), bf16[128,2048]{1,0:T(8,128)(2,1)}) %reduce-scatter.3.cloned.1.call-update) | async-done | bytes 524304 | tf_op jit(solution)/shard_map/reduce_scatter | solution.py:213
  127.8 1.5 fusion.9
  129.3 2.2 fusion.11
  131.5 10.2 %all-gather = s32[512,8]{0,1:T(8,128)S(1)} all-gather(s32[128,8]{0,1:T(8,128)S(1)} %copy-done.11), channel_id=2, replica_groups=mesh['attn'=8,'expert'=4] {'expert'}, dimensions={0}, use_global_device_ids=true | all-gather | bytes 20480 | tf_op jit(solution)/shard_map/all_gather | solution.py:184
  142.0 35.1 %all-gather.5.cloned.1.call-done = bf16[512,2048]{1,0:T(8,128)(2,1)} async-done(((bf16[128,2048]{1,0:T(8,128)(2,1)}), bf16[512,2048]{1,0:T(8,128)(2,1)}) %all-gather.5.cloned.1.call-update) | async-done | bytes 2097168 | tf_op jit(solution)/shard_map/all_gather | solution.py:222
  177.1 3.4 convert_bitcast_fusion
  180.5 1.1 copy.36
  181.6 73.7 %all_to_all.30 = bf16[8,4,48,2048]{3,2,1,0:T(8,128)(2,1)S(1)} all-to-all(bf16[8,4,48,2048]{3,2,1,0:T(8,128)(2,1)S(1)} %copy.36), channel_id=1, replica_groups=mesh['attn'=8,'expert'=4] {'attn'}, dimensions={0} | all-to-all | bytes 12582912 | tf_op jit(solution)/shard_map/all_to_all | solution.py:226
  255.3 5.2 %fusion.6 = f32[1536,768]{1,0:T(8,128)S(1)} fusion(bf16[1536,2048]{1,0:T(8,128)(2,1)S(1)} %bitcast.55, bf16[1,2048,768]{2,1,0:T(8,128)(2,1)S(1)} %copy-done.13), kind=kOutput, calls=%fused_computation.8 | convolution fusion | flops 4831838208 | bytes 14155776 | tf_op jit(solution)/shard_map/dot_general | solution.py:228
  260.5 5.6 %multiply_convert_fusion = bf16[1536,768]{1,0:T(8,128)(2,1)S(1)} fusion(f32[1536,768]{1,0:T(8,128)S(1)} %fusion.6, bf16[1536,2048]{1,0:T(8,128)(2,1)S(1)} %bitcast.56, bf16[1,2048,768]{2,1,0:T(8,128)(2,1)S(1)} %copy-done.14), kind=kOutput, calls=%fused_computation.4 | convolution fusion | flops 4838916096 | bytes 16515072 | tf_op jit(solution)/shard_map/dot_general | solution.py:229
  266.2 7.1 %convolution_convert_fusion = bf16[1536,2048]{1,0:T(8,128)(2,1)} fusion(bf16[1536,768]{1,0:T(8,128)(2,1)S(1)} %multiply_convert_fusion, bf16[1,768,2048]{2,1,0:T(8,128)(2,1)S(1)} %copy-done), kind=kOutput, calls=%fused_computation | convolution fusion | flops 4834983936 | bytes 11796480 | tf_op jit(solution)/shard_map/dot_general | solution.py:232
  273.2 7.2 %all-to-all-start.2 = ((bf16[8,4,48,2048]{3,2,1,0:T(8,128)(2,1)}), bf16[8,4,48,2048]{3,2,1,0:T(8,128)(2,1)}, u32[]{:S(2)}, u32[]{:S(2)}) async-start(bf16[8,4,48,2048]{3,2,1,0:T(8,128)(2,1)} %bitcast.54), calls=%async_computation.3 | async-start | bytes 12582912 | tf_op jit(solution)/shard_map/all_to_all | solution.py:231
  280.5 10.2 %all-gather.1 = f32[512,8]{0,1:T(8,128)S(1)} all-gather(f32[128,8]{0,1:T(8,128)S(1)} %broadcast_divide_fusion), channel_id=3, replica_groups=mesh['attn'=8,'expert'=4] {'expert'}, dimensions={0}, use_global_device_ids=true | all-gather | bytes 20480 | tf_op jit(solution)/shard_map/all_gather | solution.py:185
  290.8 57.4 %all-to-all-done.2 = bf16[8,4,48,2048]{3,2,1,0:T(8,128)(2,1)} async-done(((bf16[8,4,48,2048]{3,2,1,0:T(8,128)(2,1)}), bf16[8,4,48,2048]{3,2,1,0:T(8,128)(2,1)}, u32[]{:S(2)}, u32[]{:S(2)}) %all-to-all-start.2) | async-done | bytes 6291488 | tf_op jit(solution)/shard_map/all_to_all | solution.py:231
  348.3 5.5 %bitcast_convert_fusion = bf16[4,128,2048]{2,1,0:T(8,128)(2,1)} fusion(bf16[8,4,48,2048]{3,2,1,0:T(8,128)(2,1)} %all-to-all-done.2, bf16[4,8,128]{2,1,0:T(8,128)(2,1)S(1)} %fusion.17, s32[4,8,128]{2,1,0:T(8,128)S(1)} %fusion.8), kind=kOutput, calls=%fused_computation.5 | convolution fusion | flops 806748160 | bytes 8413184 | tf_op jit(solution)/shard_map/eacr,aecd->erd/dot_general | solution.py:240
  353.8 43.8 %reduce-scatter.5.cloned.1.call-done = bf16[1,128,2048]{2,1,0:T(8,128)(2,1)} async-done(((bf16[4,128,2048]{2,1,0:T(8,128)(2,1)}), bf16[1,128,2048]{2,1,0:T(8,128)(2,1)}) %reduce-scatter.5.cloned.1.call-update) | async-done | bytes 524304 | tf_op jit(solution)/shard_map/reduce_scatter | solution.py:243
  397.6 2.4 fusion.12
  (41 shorter events, 4.4 us)
Async XLA Ops:
  6.5 259.6 %copy-start = (bf16[1,768,2048]{2,1,0:T(8,128)(2,1)S(1)}, bf16[1,768,2048]{2,1,0:T(8,128)(2,1)}, u32[]{:S(2)}) copy-start(bf16[1,768,2048]{2,1,0:T(8,128)(2,1)} %param.33) | copy-start | bytes 9437188
  6.5 121.3 %reduce-scatter.3.cloned.1.call-start = ((), (), s32[]{:S(2)}) async-start(), calls=%async_computation.5 | async-start | bytes 2621440 | tf_op jit(solution)/shard_map/reduce_scatter | solution.py:213
  8.3 0.7 copy-start.1
  8.9 2.2 copy-start.2
  11.1 2.2 copy-start.3
  13.3 1.2 copy-start.4
  14.5 0.9 copy-start.5
  15.4 0.9 copy-start.6
  16.3 0.7 copy-start.7
  17.0 0.7 copy-start.8
  51.3 30.7 %copy-start.12 = (bf16[1024,2048]{1,0:T(8,128)(2,1)S(1)}, bf16[1024,2048]{1,0:T(8,128)(2,1)}, u32[]{:S(2)}) copy-start(bf16[1024,2048]{1,0:T(8,128)(2,1)} %param.27) | copy-start | bytes 12582916
  82.1 47.2 %copy-start.10 = (f32[2048]{0:T(1024)S(1)}, f32[2048]{0:T(1024)}, u32[]{:S(2)}) copy-start(f32[2048]{0:T(1024)} %param.28) | copy-start | bytes 24580
  85.8 45.7 %copy-start.11 = (s32[128,8]{0,1:T(8,128)S(1)}, s32[128,8]{0,1:T(8,128)}, u32[]{:S(2)}) copy-start(s32[128,8]{0,1:T(8,128)} %param.29) | copy-start | bytes 12292
  85.8 91.3 %all-gather.5.cloned.1.call-start = ((), (), s32[]{:S(2)}) async-start(), calls=%async_computation.7 | async-start | bytes 2621440 | tf_op jit(solution)/shard_map/all_gather | solution.py:222
  181.6 73.7 %copy-start.13 = (bf16[1,2048,768]{2,1,0:T(8,128)(2,1)S(1)}, bf16[1,2048,768]{2,1,0:T(8,128)(2,1)}, u32[]{:S(2)}) copy-start(bf16[1,2048,768]{2,1,0:T(8,128)(2,1)} %param.31) | copy-start | bytes 9437188
  255.3 5.2 %copy-start.14 = (bf16[1,2048,768]{2,1,0:T(8,128)(2,1)S(1)}, bf16[1,2048,768]{2,1,0:T(8,128)(2,1)}, u32[]{:S(2)}) copy-start(bf16[1,2048,768]{2,1,0:T(8,128)(2,1)} %param.32) | copy-start | bytes 9437188
  273.2 7.2 %copy-start.9 = (f32[128,8]{0,1:T(8,128)S(1)}, f32[128,8]{0,1:T(8,128)}, u32[]{:S(2)}) copy-start(f32[128,8]{0,1:T(8,128)} %param.30) | copy-start | bytes 12292
  273.2 75.0 %all-to-all-start.2 = ((bf16[8,4,48,2048]{3,2,1,0:T(8,128)(2,1)}), bf16[8,4,48,2048]{3,2,1,0:T(8,128)(2,1)}, u32[]{:S(2)}, u32[]{:S(2)}) async-start(bf16[8,4,48,2048]{3,2,1,0:T(8,128)(2,1)} %bitcast.54), calls=%async_computation.3 | async-start | bytes 12582912 | tf_op jit(solution)/shard_map/all_to_all | solution.py:231
  280.4 117.2 %reduce-scatter.5.cloned.1.call-start = ((), (), s32[]{:S(2)}) async-start(), calls=%async_computation.6 | async-start | bytes 2621440 | tf_op jit(solution)/shard_map/reduce_scatter | solution.py:243
Sparse Core Ops, SparseCore 0:
  85.9 41.8 reduce-scatter.2
  131.6 45.4 all-gather.4
  353.9 43.6 reduce-scatter.4

commit v2 on v1

--- a/solution.py
+++ b/solution.py
@@ -152,6 +152,222 @@
     )
 
 
+def experts_kernel(
+    residual_ref,
+    normed_ref,
+    select_ref,
+    combine_ref,
+    gate_ref,
+    up_ref,
+    down_ref,
+    out_ref,
+    column,
+    outbox,
+    inbox,
+    returned,
+    partial,
+    summed,
+    column_send,
+    column_recv,
+    out_send,
+    out_recv,
+    back_send,
+    back_recv,
+    sum_send,
+    sum_recv,
+):
+    planes, places, capacity, model_width = inbox.shape
+    me = lax.axis_index("attn")
+    plane = lax.axis_index("expert")
+
+    def other_plane(step):
+        return lax.rem(plane + step, planes)
+
+    def other_place(step):
+        return lax.rem(me + step, places)
+
+    def column_copy(source, target, owner):
+        return pltpu.make_async_remote_copy(
+            src_ref=normed_ref,
+            dst_ref=column.at[owner],
+            send_sem=column_send.at[target],
+            recv_sem=column_recv.at[owner],
+            device_id=(me, source),
+            device_id_type=pl.DeviceIdType.MESH,
+        )
+
+    def out_copy(block, target, owner):
+        return pltpu.make_async_remote_copy(
+            src_ref=outbox.at[block, target],
+            dst_ref=inbox.at[block, owner],
+            send_sem=out_send.at[block, target],
+            recv_sem=out_recv.at[block, owner],
+            device_id=(target, plane),
+            device_id_type=pl.DeviceIdType.MESH,
+        )
+
+    def back_copy(block, target, owner):
+        return pltpu.make_async_remote_copy(
+            src_ref=inbox.at[block, target],
+            dst_ref=returned.at[block, owner],
+            send_sem=back_send.at[block, target],
+            recv_sem=back_recv.at[block, owner],
+            device_id=(target, plane),
+            device_id_type=pl.DeviceIdType.MESH,
+        )
+
+    def sum_copy(target, owner):
+        return pltpu.make_async_remote_copy(
+            src_ref=partial.at[target],
+            dst_ref=summed.at[owner],
+            send_sem=sum_send.at[target],
+            recv_sem=sum_recv.at[owner],
+            device_id=(me, target),
+            device_id_type=pl.DeviceIdType.MESH,
+        )
+
+    barrier = pltpu.get_barrier_semaphore()
+
+    @pl.loop(1, planes)
+    def _(step):
+        pl.semaphore_signal(
+            barrier,
+            inc=1,
+            device_id=(me, other_plane(step)),
+            device_id_type=pl.DeviceIdType.MESH,
+        )
+
+    @pl.loop(1, places)
+    def _(step):
+        pl.semaphore_signal(
+            barrier,
+            inc=1,
+            device_id=(other_place(step), plane),
+            device_id_type=pl.DeviceIdType.MESH,
+        )
+
+    pl.semaphore_wait(barrier, planes + places - 2)
+
+    @pl.loop(1, planes)
+    def _(step):
+        target = other_plane(step)
+        column_copy(target, target, plane).start()
+
+    column[plane] = normed_ref[...]
+
+    def dispatch(block):
+        def rows_for(place):
+            return jnp.dot(
+                select_ref[block, place], column[block], preferred_element_type=jnp.float32
+            ).astype(jnp.bfloat16)
+
+        @pl.loop(1, places)
+        def _(step):
+            target = other_place(step)
+            outbox[block, target] = rows_for(target)
+            out_copy(block, target, me).start()
+
+        inbox[block, me] = rows_for(me)
+
+    dispatch(plane)
+
+    @pl.loop(1, planes)
+    def _(step):
+        block = other_plane(planes - step)
+        column_copy(block, block, block).wait_recv()
+        dispatch(block)
+
+    @pl.loop(1, planes + 1)
+    def _(step):
+        block = other_plane(planes - lax.rem(step, planes))
+
+        @pl.loop(1, places)
+        def _(turn):
+            owner = other_place(turn)
+            out_copy(block, owner, owner).wait_recv()
+
+        rows = inbox[block].reshape(places * capacity, model_width)
+        gate_part = jnp.dot(rows, gate_ref[...], preferred_element_type=jnp.float32)
+        up_part = jnp.dot(rows, up_ref[...], preferred_element_type=jnp.float32)
+        activated = (gate_part / (1.0 + jnp.exp(-gate_part)) * up_part).astype(jnp.bfloat16)
+        inbox[block] = (
+            jnp.dot(activated, down_ref[...], preferred_element_type=jnp.float32)
+            .astype(jnp.bfloat16)
+            .reshape(places, capacity, model_width)
+        )
+
+        @pl.loop(1, places)
+        def _(turn):
+            back_copy(block, other_place(turn), me).start()
+
+        returned[block, me] = inbox[block, me]
+
+    def combined(block):
+        @pl.loop(1, places)
+        def _(turn):
+            owner = other_place(turn)
+            back_copy(block, owner, owner).wait_recv()
+
+        return jnp.dot(
+            combine_ref[block],
+            returned[block].reshape(places * capacity, model_width),
+            preferred_element_type=jnp.float32,
+        )
+
+    @pl.loop(1, planes)
+    def _(step):
+        block = other_plane(planes - step)
+        partial[block] = combined(block).astype(jnp.bfloat16)
+        sum_copy(block, plane).start()
+
+    total = residual_ref[...].astype(jnp.float32) + combined(plane)
+    for step in range(1, planes):
+        owner = other_plane(step)
+        sum_copy(owner, owner).wait_recv()
+        total = total + summed[owner].astype(jnp.float32)
+    out_ref[...] = total.astype(jnp.bfloat16)
+
+    @pl.loop(1, planes)
+    def _(step):
+        target = other_plane(step)
+        column_copy(target, target, plane).wait_send()
+        sum_copy(target, plane).wait_send()
+
+    @pl.loop(0, planes)
+    def _(block):
+        @pl.loop(1, places)
+        def _(turn):
+            target = other_place(turn)
+            out_copy(block, target, me).wait_send()
+            back_copy(block, target, me).wait_send()
+
+
+def mix_experts(residual, normed, select, combine, gate_matrix, up_matrix, down_matrix):
+    planes, places, capacity, answer_rows = select.shape
+    model_width = normed.shape[1]
+    box = pltpu.VMEM((planes, places, capacity, model_width), jnp.bfloat16)
+    blocks = pltpu.VMEM((planes, answer_rows, model_width), jnp.bfloat16)
+    per_plane = pltpu.SemaphoreType.DMA((planes,))
+    per_pair = pltpu.SemaphoreType.DMA((planes, places))
+    return pl.pallas_call(
+        experts_kernel,
+        out_shape=jax.ShapeDtypeStruct(residual.shape, jnp.bfloat16),
+        in_specs=[pl.BlockSpec(memory_space=pltpu.VMEM)] * 7,
+        out_specs=pl.BlockSpec(memory_space=pltpu.VMEM),
+        scratch_shapes=[box_shape for box_shape in (blocks, box, box, box, blocks, blocks)]
+        + [per_plane, per_plane, per_pair, per_pair, per_pair, per_pair, per_plane, per_plane],
+        compiler_params=pltpu.CompilerParams(
+            collective_id=0, has_side_effects=True, vmem_limit_bytes=60 * 2**20
+        ),
+        cost_estimate=pl.CostEstimate(
+            flops=6 * planes * places * capacity * gate_matrix.size,
+            bytes_accessed=6 * gate_matrix.size,
+            transcendentals=0,
+        ),
+        name="mix_experts",
+    )(residual, normed, select, combine, gate_matrix, up_matrix, down_matrix)
+
+
 def on_device(
     hidden,
     queries,
@@ -219,29 +435,18 @@
     residual = (hidden.astype(jnp.float32) + projected).astype(jnp.bfloat16)
     normed = rms_scaled(residual.astype(jnp.float32), post_gain).astype(jnp.bfloat16)
 
-    column = lax.all_gather(normed, "expert")
-    outgoing = jnp.einsum(
-        "eacr,erd->aecd", select, column, preferred_element_type=jnp.float32
-    ).astype(jnp.bfloat16)
-    arrived = lax.all_to_all(outgoing, "attn", split_axis=0, concat_axis=0, tiled=True)
-    flat_rows = arrived.reshape(-1, model_width)
-    gate_part = jnp.dot(flat_rows, expert_gate[0], preferred_element_type=jnp.float32)
-    up_part = jnp.dot(flat_rows, expert_up[0], preferred_element_type=jnp.float32)
-    activated = (jax.nn.silu(gate_part) * up_part).astype(jnp.bfloat16)
-    returned = lax.all_to_all(
-        jnp.dot(activated, expert_down[0], preferred_element_type=jnp.float32)
-        .astype(jnp.bfloat16)
-        .reshape(arrived.shape),
-        "attn",
-        split_axis=0,
-        concat_axis=0,
-        tiled=True,
-    )
-    partial = jnp.einsum(
-        "eacr,aecd->erd", combine, returned, preferred_element_type=jnp.float32
-    ).astype(jnp.bfloat16)
-    mixture = lax.psum_scatter(partial, "expert", scatter_dimension=0, tiled=True)[0]
-    return (residual.astype(jnp.float32) + mixture.astype(jnp.float32)).astype(jnp.bfloat16)
+    combine = combine.transpose(0, 3, 1, 2).reshape(
+        expert_count, answer_rows, attn_count * capacity
+    )
+    return mix_experts(
+        residual,
+        normed,
+        select,
+        combine,
+        expert_gate[0],
+        expert_up[0],
+        expert_down[0],
+    )
 
 
 def solution(mesh):

time: 409 us -> 300 us (0.73)
  waiting for transfers between devices: 178 us -> 18.4 us
  Pallas kernels: 33.7 us -> 168 us
  blocking collectives: 125 us -> 78.2 us
  matrix products: 30.6 us -> 3.83 us
  starting transfers between devices: 7.24 us -> 0.01 us
    pallas_call x0 -> x1, Pallas kernels: none -> 160 us  [mix_experts(): pl.pallas_call(experts_kernel, out_shape=jax.ShapeDtypeStruct(residual.sh...]
    all_to_all x1 -> x0, blocking collectives: 73.7 us -> none  [on_device(): lax.all_to_all(outgoing, 'attn', split_axis=0, concat_axis=0, tiled=True)]
    all_to_all x1 -> x0, waiting for transfers between devices: 57.4 us -> none  [on_device(): lax.all_to_all(jnp.dot(activated, expert_down[0], preferred_element_type=...]
    reduce_scatter x1 -> x0, waiting for transfers between devices: 43.8 us -> none  [on_device(): lax.psum_scatter(partial, 'expert', scatter_dimension=0, tiled=True)[0]]
    all_gather x1 -> x0, waiting for transfers between devices: 35.1 us -> none  [on_device(): column = lax.all_gather(normed, 'expert')]
    dot_general x5 -> x0, matrix products: 26.7 us -> none  [the longest x1 7.08 us: on_device(): jnp.dot(activated, expert_down[0], preferred_element_type=jnp.float32)]
    pallas_call x1, Pallas kernels: 33.7 us -> 8.26 us  [attend(): pl.pallas_call(functools.partial(attention_kernel, key_block), out_shape=...]
    all_to_all x1, blocking collectives: 30.6 us -> 56.1 us  [on_device(): lax.all_to_all(attended, 'expert', split_axis=1, concat_axis=0, tiled=True)]
  transfers between devices with their start and end apart: 4 -> 1, of which waited for: 4 -> 1; matrix products, arithmetic and copies ran while one was open for 0% -> 1% of each run, Pallas kernels for 0% -> 0%
where the time goes in v2:
time: 300 us
  Pallas kernels  168 us (56%)
  blocking collectives  78.2 us (26%)
  waiting for transfers between devices  18.4 us (6%)
  between operations  14.2 us (5%)
  local copies, waits for them, and re-layouts  12.8 us (4%)
  other arithmetic  4.25 us (1%)
  matrix products  3.83 us (1%)
    pallas_call x1, Pallas kernels, mix_experts(): pl.pallas_call(experts_kernel, out_shape=jax.ShapeDtypeStruct(residual.sh...  160 us
    all_to_all x1, blocking collectives, on_device(): lax.all_to_all(attended, 'expert', split_axis=1, concat_axis=0, tiled=True)  56.1 us
    reduce_scatter x1, waiting for transfers between devices, on_device(): lax.psum_scatter(jnp.dot(swapped, out_proj, preferred_element_type=jnp.fl...  18.4 us
    all_gather x1, blocking collectives, on_device(): shares = lax.all_gather(gate_share, 'expert')  11.4 us
    unnamed x29, local copies, waits for them, and re-layouts  11.3 us
    all_gather x1, blocking collectives, on_device(): ids = lax.all_gather(route_ids, 'expert')  10.7 us
    pallas_call x1, Pallas kernels, attend(): pl.pallas_call(functools.partial(attention_kernel, key_block), out_shape=...  8.26 us
  transfers between devices with their start and end apart: 1, of which 1 were waited for; matrix products, arithmetic and copies ran while one was open for 1% of the time, Pallas kernels for 0%

profile of v2, /device:TPU:5, one launch (start us, length us, event | category | flops | bytes accessed | tf_op | source)
XLA Modules:
  0.0 300.1 jit_solution(7039164277400963750)
XLA Ops:
  7.2 0.8 copy.28.option_column_ref
  8.0 0.6 copy-done
  8.6 2.2 copy-done.1
  10.8 2.2 copy-done.2
  13.0 1.2 copy-done.3
  14.2 0.9 copy-done.4
  15.1 0.9 copy-done.5
  16.0 0.7 copy-done.6
  16.7 0.7 copy-done.7
  17.3 8.3 %attend.1 = bf16[128,4096]{1,0:T(8,128)(2,1)S(1)} custom-call(s32[1]{0:T(128)S(6)} %copy.36.length_ref, bf16[128,4096]{1,0:T(8,128)(2,1)S(1)} %copy-done.3, bf16[128,512]{1,0:T(8,128)(2,1)S(1)} %copy-done.4, bf16[128,512]{1,0:T(8,128)(2,1)S(1)} %copy-done.5, bf16[4096,512]{1,0:T(8,128)(2,1)S(1)} %bitcast.29, bf16[4096,512]{1,0:T(8,128)(2,1)S(1)} %bitcast.30, ...), custom_call_target="tpu_custom_call" | custom-call | flops 8589934592 | bytes 8388608 | tf_op jit(solution)/shard_map/attend/pallas_call | solution.py:111
  25.7 56.1 %all_to_all.19 = bf16[128,4,1024]{2,0,1:T(8,128)(2,1)S(1)} all-to-all(bf16[128,4,1024]{2,0,1:T(8,128)(2,1)S(1)} %bitcast.33), channel_id=1, replica_groups=mesh['attn'=8,'expert'=4] {'expert'}, dimensions={1} | all-to-all | bytes 2097152 | tf_op jit(solution)/shard_map/all_to_all | solution.py:428
  81.8 3.7 %convolution_convert_fusion = bf16[512,2048]{1,0:T(8,128)(2,1)} fusion(bf16[512,1024]{1,0:T(8,128)(2,1)S(1)} %bitcast.36, bf16[1024,2048]{1,0:T(8,128)(2,1)S(1)} %copy-done.13), kind=kOutput, calls=%fused_computation | convolution fusion | flops 2148532224 | bytes 7340032 | tf_op jit(solution)/shard_map/dot_general | solution.py:430
  85.5 10.7 %all-gather = s32[512,8]{0,1:T(8,128)S(1)} all-gather(s32[128,8]{0,1:T(8,128)S(1)} %copy-done.12), channel_id=2, replica_groups=mesh['attn'=8,'expert'=4] {'expert'}, dimensions={0}, use_global_device_ids=true | all-gather | bytes 20480 | tf_op jit(solution)/shard_map/all_gather | solution.py:400
  96.2 11.4 %all-gather.1 = f32[512,8]{0,1:T(8,128)S(1)} all-gather(f32[128,8]{0,1:T(8,128)S(1)} %broadcast_divide_fusion), channel_id=3, replica_groups=mesh['attn'=8,'expert'=4] {'expert'}, dimensions={0}, use_global_device_ids=true | all-gather | bytes 20480 | tf_op jit(solution)/shard_map/all_gather | solution.py:401
  107.8 0.2 copy.31
  108.2 0.1 fusion
  108.4 0.3 copy.30
  108.8 0.8 fusion.4.select_ref
  109.6 0.9 select_convert_fusion.combine_ref
  110.5 18.4 %reduce-scatter.2.cloned.1.call-done = bf16[128,2048]{1,0:T(8,128)(2,1)} async-done(((bf16[512,2048]{1,0:T(8,128)(2,1)}), bf16[128,2048]{1,0:T(8,128)(2,1)}) %reduce-scatter.2.cloned.1.call-update) | async-done | bytes 524304 | tf_op jit(solution)/shard_map/reduce_scatter | solution.py:429
  128.9 1.3 fusion.1
  130.2 1.0 fusion.3.normed_ref
  131.2 160.1 %mix_experts.1 = bf16[128,2048]{1,0:T(8,128)(2,1)} custom-call(bf16[128,2048]{1,0:T(8,128)(2,1)} %copy-done.8, bf16[128,2048]{1,0:T(8,128)(2,1)} %fusion.3.normed_ref, bf16[4,8,48,128]{3,2,1,0:T(8,128)(2,1)} %fusion.4.select_ref, bf16[4,128,384]{2,1,0:T(8,128)(2,1)} %select_convert_fusion.combine_ref, bf16[2048,768]{1,0:T(8,128)(2,1)} %bitcast.42, ...), custom_call_target="tpu_custom_call" | custom-call | flops 14495514624 | bytes 9437184 | tf_op jit(solution)/shard_map/mix_experts/pallas_call | solution.py:352
  291.3 1.9 copy.37
  (33 shorter events, 0.6 us)
Async XLA Ops:
  6.5 122.3 %reduce-scatter.2.cloned.1.call-start = ((), (), s32[]{:S(2)}) async-start(), calls=%async_computation.2 | async-start | bytes 2621440 | tf_op jit(solution)/shard_map/reduce_scatter | solution.py:429
  8.0 0.7 copy-start
  8.6 2.2 copy-start.1
  10.8 2.2 copy-start.2
  13.0 1.2 copy-start.3
  14.2 0.9 copy-start.4
  15.1 0.9 copy-start.5
  16.0 0.7 copy-start.6
  16.7 0.7 copy-start.7
  25.6 56.2 %copy-start.13 = (bf16[1024,2048]{1,0:T(8,128)(2,1)S(1)}, bf16[1024,2048]{1,0:T(8,128)(2,1)}, u32[]{:S(2)}) copy-start(bf16[1024,2048]{1,0:T(8,128)(2,1)} %param.27) | copy-start | bytes 12582916
  81.8 3.7 %copy-start.10 = (f32[128,8]{0,1:T(8,128)S(1)}, f32[128,8]{0,1:T(8,128)}, u32[]{:S(2)}) copy-start(f32[128,8]{0,1:T(8,128)} %param.30) | copy-start | bytes 12292
  81.8 3.8 %copy-start.12 = (s32[128,8]{0,1:T(8,128)S(1)}, s32[128,8]{0,1:T(8,128)}, u32[]{:S(2)}) copy-start(s32[128,8]{0,1:T(8,128)} %param.29) | copy-start | bytes 12292
  85.5 43.4 %copy-start.9 = (bf16[128,2048]{1,0:T(8,128)(2,1)S(1)}, bf16[128,2048]{1,0:T(8,128)(2,1)}, u32[]{:S(2)}) copy-start(bf16[128,2048]{1,0:T(8,128)(2,1)} %param.17) | copy-start | bytes 1572868
  85.5 44.8 %copy-start.11 = (f32[2048]{0:T(1024)S(1)}, f32[2048]{0:T(1024)}, u32[]{:S(2)}) copy-start(f32[2048]{0:T(1024)} %param.28) | copy-start | bytes 24580
  130.2 1.0 copy-start.8
Sparse Core Ops, SparseCore 0:
  85.6 43.2 reduce-scatter.1

commit v3 on v2

--- a/solution.py
+++ b/solution.py
@@ -155,18 +155,20 @@
 def experts_kernel(
     residual_ref,
     normed_ref,
-    select_ref,
-    combine_ref,
+    routing_ref,
     gate_ref,
     up_ref,
     down_ref,
     out_ref,
+    routing,
     column,
     outbox,
     inbox,
     returned,
     partial,
     summed,
+    routing_send,
+    routing_recv,
     column_send,
     column_recv,
     out_send,
@@ -186,6 +188,16 @@
     def other_place(step):
         return lax.rem(me + step, places)
 
+    def routing_copy(target, owner):
+        return pltpu.make_async_remote_copy(
+            src_ref=routing_ref.at[target],
+            dst_ref=routing.at[owner],
+            send_sem=routing_send.at[target],
+            recv_sem=routing_recv.at[owner],
+            device_id=(me, target),
+            device_id_type=pl.DeviceIdType.MESH,
+        )
+
     def column_copy(source, target, owner):
         return pltpu.make_async_remote_copy(
             src_ref=normed_ref,
@@ -251,15 +263,20 @@
     @pl.loop(1, planes)
     def _(step):
         target = other_plane(step)
+        routing_copy(target, plane).start()
         column_copy(target, target, plane).start()
 
+    routing[plane] = routing_ref[plane]
     column[plane] = normed_ref[...]
+    answer_rows = normed_ref.shape[0]
+    slots = lax.broadcasted_iota(jnp.int32, (capacity, answer_rows), 0).astype(jnp.float32)
 
     def dispatch(block):
         def rows_for(place):
-            return jnp.dot(
-                select_ref[block, place], column[block], preferred_element_type=jnp.float32
-            ).astype(jnp.bfloat16)
+            select = jnp.where(routing[block, place] == slots, 1.0, 0.0).astype(jnp.bfloat16)
+            return jnp.dot(select, column[block], preferred_element_type=jnp.float32).astype(
+                jnp.bfloat16
+            )
 
         @pl.loop(1, places)
         def _(step):
@@ -274,6 +291,7 @@
     @pl.loop(1, planes)
     def _(step):
         block = other_plane(planes - step)
+        routing_copy(block, block).wait_recv()
         column_copy(block, block, block).wait_recv()
         dispatch(block)
 
@@ -308,8 +326,15 @@
             owner = other_place(turn)
             back_copy(block, owner, owner).wait_recv()
 
+        shares = jnp.concatenate(
+            [
+                jnp.where(routing[block, place] == slots, routing[block, places + place], 0.0)
+                for place in range(places)
+            ],
+            axis=0,
+        )
         return jnp.dot(
-            combine_ref[block],
+            shares.T.astype(jnp.bfloat16),
             returned[block].reshape(places * capacity, model_width),
             preferred_element_type=jnp.float32,
         )
@@ -330,6 +355,7 @@
     @pl.loop(1, planes)
     def _(step):
         target = other_plane(step)
+        routing_copy(target, plane).wait_send()
         column_copy(target, target, plane).wait_send()
         sum_copy(target, plane).wait_send()
 
@@ -342,9 +368,9 @@
             back_copy(block, target, me).wait_send()
 
 
-def mix_experts(residual, normed, select, combine, gate_matrix, up_matrix, down_matrix):
-    planes, places, capacity, answer_rows = select.shape
-    model_width = normed.shape[1]
+def mix_experts(residual, normed, routing, capacity, gate_matrix, up_matrix, down_matrix):
+    planes, places = routing.shape[0], routing.shape[1] // 2
+    answer_rows, model_width = normed.shape
     box = pltpu.VMEM((planes, places, capacity, model_width), jnp.bfloat16)
     blocks = pltpu.VMEM((planes, answer_rows, model_width), jnp.bfloat16)
     per_plane = pltpu.SemaphoreType.DMA((planes,))
@@ -352,10 +378,11 @@
     return pl.pallas_call(
         experts_kernel,
         out_shape=jax.ShapeDtypeStruct(residual.shape, jnp.bfloat16),
-        in_specs=[pl.BlockSpec(memory_space=pltpu.VMEM)] * 7,
+        in_specs=[pl.BlockSpec(memory_space=pltpu.VMEM)] * 6,
         out_specs=pl.BlockSpec(memory_space=pltpu.VMEM),
-        scratch_shapes=[box_shape for box_shape in (blocks, box, box, box, blocks, blocks)]
-        + [per_plane, per_plane, per_pair, per_pair, per_pair, per_pair, per_plane, per_plane],
+        scratch_shapes=[pltpu.VMEM(routing.shape, jnp.float32)]
+        + [blocks, box, box, box, blocks, blocks]
+        + [per_plane, per_plane, per_plane, per_plane, per_pair, per_pair, per_pair, per_pair, per_plane, per_plane],
         compiler_params=pltpu.CompilerParams(
             collective_id=0, has_side_effects=True, vmem_limit_bytes=60 * 2**20
         ),
@@ -365,7 +392,7 @@
             transcendentals=0,
         ),
         name="mix_experts",
-    )(residual, normed, select, combine, gate_matrix, up_matrix, down_matrix)
+    )(residual, normed, routing, gate_matrix, up_matrix, down_matrix)
 
 
 def on_device(
@@ -394,25 +421,19 @@
     device_count = attn_count * expert_count
     capacity = 3 * answer_rows * top_count // (2 * device_count)
     capacity = (capacity + 15) // 16 * 16
-    plane = lax.axis_index("expert")
 
     gate_share = route_weights / jnp.sum(route_weights, axis=1, keepdims=True)
-    ids = lax.all_gather(route_ids, "expert")
-    shares = lax.all_gather(gate_share, "expert")
-    plane_experts = jnp.arange(attn_count, dtype=jnp.int32) * expert_count + plane
-    chosen = ids[:, None, :, :] == plane_experts[None, :, None, None]
-    share = jnp.sum(jnp.where(chosen, shares[:, None, :, :], 0.0), axis=-1)
+    experts = jnp.arange(device_count, dtype=jnp.int32).reshape(attn_count, expert_count).T
+    chosen = route_ids[None, None, :, :] == experts[:, :, None, None]
+    share = jnp.sum(jnp.where(chosen, gate_share[None, None, :, :], 0.0), axis=-1)
     hit = jnp.any(chosen, axis=-1)
-    earlier = (
-        jnp.arange(answer_rows)[:, None] < jnp.arange(answer_rows)[None, :]
-    ).astype(jnp.bfloat16)
+    positions = jnp.arange(answer_rows)
+    earlier = (positions[:, None] < positions[None, :]).astype(jnp.bfloat16)
     rank = jnp.einsum(
         "ear,rs->eas", hit.astype(jnp.bfloat16), earlier, preferred_element_type=jnp.float32
-    ).astype(jnp.int32)
-    slot = jnp.where(hit, rank, -1)
-    picks = slot[:, :, None, :] == jnp.arange(capacity, dtype=jnp.int32)[None, None, :, None]
-    select = picks.astype(jnp.bfloat16)
-    combine = jnp.where(picks, share[:, :, None, :], 0.0).astype(jnp.bfloat16)
+    )
+    slot = jnp.where(hit, rank, -1.0)
+    routing = jnp.concatenate([slot, share], axis=1)[:, :, None, :]
 
     attended = attend(
         queries,
@@ -435,14 +456,11 @@
     residual = (hidden.astype(jnp.float32) + projected).astype(jnp.bfloat16)
     normed = rms_scaled(residual.astype(jnp.float32), post_gain).astype(jnp.bfloat16)
 
-    combine = combine.transpose(0, 3, 1, 2).reshape(
-        expert_count, answer_rows, attn_count * capacity
-    )
     return mix_experts(
         residual,
         normed,
-        select,
-        combine,
+        routing,
+        capacity,
         expert_gate[0],
         expert_up[0],
         expert_down[0],

time: 300 us -> 300 us (level)
  blocking collectives: 78.2 us -> 36.8 us
  waiting for transfers between devices: 18.4 us -> 43 us
  Pallas kernels: 168 us -> 187 us
    reduce_scatter x1, waiting for transfers between devices: 18.4 us -> 43 us  [on_device(): lax.psum_scatter(jnp.dot(swapped, out_proj, preferred_element_type=jnp.fl...]
    all_gather x2 -> x0, blocking collectives: 22.1 us -> none  [the longest x1 11.4 us: on_device(): shares = lax.all_gather(gate_share, 'expert')]
    all_to_all x1, blocking collectives: 56.1 us -> 36.8 us  [on_device(): lax.all_to_all(attended, 'expert', split_axis=1, concat_axis=0, tiled=True)]
    pallas_call x1, Pallas kernels: 8.26 us -> 26.4 us  [attend(): pl.pallas_call(functools.partial(attention_kernel, key_block), out_shape=...]
  transfers between devices with their start and end apart: 1 -> 1, of which waited for: 1 -> 1; matrix products, arithmetic and copies ran while one was open for 1% -> 0% of each run, Pallas kernels for 0% -> 0%
where the time goes in v3:
time: 300 us
  Pallas kernels  187 us (62%)
  waiting for transfers between devices  43 us (14%)
  blocking collectives  36.8 us (12%)
  between operations  14.2 us (5%)
  local copies, waits for them, and re-layouts  12.1 us (4%)
  matrix products  3.83 us (1%)
  other arithmetic  3.17 us (1%)
    pallas_call x1, Pallas kernels, mix_experts(): pl.pallas_call(experts_kernel, out_shape=jax.ShapeDtypeStruct(residual.sh...  161 us
    reduce_scatter x1, waiting for transfers between devices, on_device(): lax.psum_scatter(jnp.dot(swapped, out_proj, preferred_element_type=jnp.fl...  43 us
    all_to_all x1, blocking collectives, on_device(): lax.all_to_all(attended, 'expert', split_axis=1, concat_axis=0, tiled=True)  36.8 us
    pallas_call x1, Pallas kernels, attend(): pl.pallas_call(functools.partial(attention_kernel, key_block), out_shape=...  26.4 us
    unnamed x29, local copies, waits for them, and re-layouts  11.3 us
  transfers between devices with their start and end apart: 1, of which 1 were waited for; matrix products, arithmetic and copies ran while one was open for 0% of the time, Pallas kernels for 0%

profile of v3, /device:TPU:5, one launch (start us, length us, event | category | flops | bytes accessed | tf_op | source)
XLA Modules:
  0.0 300.1 jit_solution(13632585181224022354)
XLA Ops:
  6.5 0.8 copy.25.option_column_ref
  8.0 0.6 copy-done
  8.6 2.2 copy-done.1
  10.8 2.2 copy-done.2
  13.0 1.2 copy-done.3
  14.2 0.9 copy-done.4
  15.1 0.9 copy-done.5
  16.0 0.7 copy-done.6
  16.7 0.7 copy-done.7
  17.3 26.4 %attend.1 = bf16[128,4096]{1,0:T(8,128)(2,1)S(1)} custom-call(s32[1]{0:T(128)S(6)} %copy.31.length_ref, bf16[128,4096]{1,0:T(8,128)(2,1)S(1)} %copy-done.3, bf16[128,512]{1,0:T(8,128)(2,1)S(1)} %copy-done.4, bf16[128,512]{1,0:T(8,128)(2,1)S(1)} %copy-done.5, bf16[4096,512]{1,0:T(8,128)(2,1)S(1)} %bitcast.24, bf16[4096,512]{1,0:T(8,128)(2,1)S(1)} %bitcast.25, ...), custom_call_target="tpu_custom_call" | custom-call | flops 8589934592 | bytes 8388608 | tf_op jit(solution)/shard_map/attend/pallas_call | solution.py:111
  43.8 0.0 copy-start.13
  43.8 0.1 copy.29
  43.9 36.8 %all_to_all.19 = bf16[128,4,1024]{2,0,1:T(8,128)(2,1)S(1)} all-to-all(bf16[128,4,1024]{2,0,1:T(8,128)(2,1)S(1)} %bitcast.28), channel_id=1, replica_groups=mesh['attn'=8,'expert'=4] {'expert'}, dimensions={1} | all-to-all | bytes 2097152 | tf_op jit(solution)/shard_map/all_to_all | solution.py:449
  80.7 3.7 %convolution_convert_fusion = bf16[512,2048]{1,0:T(8,128)(2,1)} fusion(bf16[512,1024]{1,0:T(8,128)(2,1)S(1)} %bitcast.29, bf16[1024,2048]{1,0:T(8,128)(2,1)S(1)} %copy-done.13), kind=kOutput, calls=%fused_computation | convolution fusion | flops 2148532224 | bytes 7340032 | tf_op jit(solution)/shard_map/dot_general | solution.py:451
  84.4 0.0 reduce-scatter.2.cloned.1.call-update
  84.5 0.1 compare_reduce_fusion
  84.6 0.1 fusion.3
  84.7 0.1 convolution_select_fusion
  84.8 0.6 pad_maximum_fusion
  85.5 43.0 %reduce-scatter.2.cloned.1.call-done = bf16[128,2048]{1,0:T(8,128)(2,1)} async-done(((bf16[512,2048]{1,0:T(8,128)(2,1)}), bf16[128,2048]{1,0:T(8,128)(2,1)}) %reduce-scatter.2.cloned.1.call-update) | async-done | bytes 524304 | tf_op jit(solution)/shard_map/reduce_scatter | solution.py:450
  128.5 1.3 fusion
  129.8 1.0 fusion.2.normed_ref
  130.8 160.6 %mix_experts.1 = bf16[128,2048]{1,0:T(8,128)(2,1)} custom-call(bf16[128,2048]{1,0:T(8,128)(2,1)} %copy-done.8, bf16[128,2048]{1,0:T(8,128)(2,1)} %fusion.2.normed_ref, f32[4,16,1,128]{3,2,1,0:T(1,128)} %bitcast.30, bf16[2048,768]{1,0:T(8,128)(2,1)} %bitcast.31, bf16[2048,768]{1,0:T(8,128)(2,1)} %bitcast.32, bf16[768,2048]{1,0:T(8,128)(2,1)} %bitcast.33), custom_call_target="tpu_custom_call" | custom-call | flops 14495514624 | bytes 9437184 | tf_op jit(solution)/shard_map/mix_experts/pallas_call | solution.py:378
  291.4 1.9 copy.32
  (24 shorter events, 0.1 us)
Async XLA Ops:
  6.5 121.9 %reduce-scatter.2.cloned.1.call-start = ((), (), s32[]{:S(2)}) async-start(), calls=%async_computation.2 | async-start | bytes 2621440 | tf_op jit(solution)/shard_map/reduce_scatter | solution.py:450
  7.9 0.7 copy-start
  8.6 2.2 copy-start.1
  10.8 2.2 copy-start.2
  13.0 1.2 copy-start.3
  14.2 0.9 copy-start.4
  15.1 0.9 copy-start.5
  16.0 0.7 copy-start.6
  16.7 0.7 copy-start.7
  43.8 36.9 %copy-start.13 = (bf16[1024,2048]{1,0:T(8,128)(2,1)S(1)}, bf16[1024,2048]{1,0:T(8,128)(2,1)}, u32[]{:S(2)}) copy-start(bf16[1024,2048]{1,0:T(8,128)(2,1)} %param.27) | copy-start | bytes 12582916
  80.7 3.7 %copy-start.10 = (f32[128,8]{0,1:T(8,128)S(1)}, f32[128,8]{0,1:T(8,128)}, u32[]{:S(2)}) copy-start(f32[128,8]{0,1:T(8,128)} %param.30) | copy-start | bytes 12292
  80.7 3.8 %copy-start.11 = (s32[128,8]{0,1:T(8,128)S(1)}, s32[128,8]{0,1:T(8,128)}, u32[]{:S(2)}) copy-start(s32[128,8]{0,1:T(8,128)} %param.29) | copy-start | bytes 12292
  80.7 47.8 %copy-start.9 = (bf16[128,2048]{1,0:T(8,128)(2,1)S(1)}, bf16[128,2048]{1,0:T(8,128)(2,1)}, u32[]{:S(2)}) copy-start(bf16[128,2048]{1,0:T(8,128)(2,1)} %param.17) | copy-start | bytes 1572868
  80.7 49.1 %copy-start.12 = (f32[2048]{0:T(1024)S(1)}, f32[2048]{0:T(1024)}, u32[]{:S(2)}) copy-start(f32[2048]{0:T(1024)} %param.28) | copy-start | bytes 24580
  129.8 1.0 copy-start.8
Sparse Core Ops, SparseCore 0:
  84.5 43.8 reduce-scatter.1
